TPU v7x, 128 devices: a whole 4x4x4 slice. The times are simulated.
128 devices in a mesh: sub: 2 (over x_hi), row: 8 (over y, core), col: 8 (over x_lo, z).
Axes of the slice: x: 4 (x_hi: 2, x_lo: 2; x = x_hi * 2 + x_lo), y: 4, z: 4, core: 2. Of those that a mesh axis runs over, the one named last changes fastest.
Arguments:
- child_fronts: float32 [2, 8192, 8192], P('sub', 'row', 'col'), as said below
- child_map: int32 [2, 56], replicated, may hold values from 0 to 95, as said below
- parent_front: float32 [12288, 12288], P(('sub', 'row'), 'col'), as said below
Outputs:
- child_factor: float32 [2, 8192, 1024], P('sub', 'row', 'col')
- parent_factor: float32 [12288, 1024], P(('sub', 'row'), 'col')
- parent_update: float32 [12288, 12288], P(('sub', 'row'), 'col')
Inputs may be any that keep to these rules, and one draw needn't show every extreme that they name: The kept blocks of child c are numbered a = 0 .. 55 in increasing order; child_map[c, a] is the parent block that receives kept block a. A child's entries are distinct. Within each run of 7 entries of one child that starts at a multiple of that length, the values child_map // 12 are distinct; for children 2h and 2h + 1 and the same run, the 2 * (7) values child_map // 6 are distinct. `child_fronts`: each front is symmetric with smallest eigenvalue above 0.05. `parent_front`: symmetric with smallest eigenvalue above 0.05.
All inputs are finite; a program needn't handle non-finite values.
Results may differ from a plain program's by a relative error of at most 0.0003.
Values sent between devices are 32-bit elements; how exact they have to be, the bound alone decides.
No kernel may reach another device: no remote copies, remote signals or barrier semaphores. Data moves between devices by JAX's collectives and lax.ppermute only.
A program may use at most 192 MiB of HBM per device.

v0:
```python
import functools

import jax
import jax.numpy as jnp
from jax import lax
from jax.experimental import pallas as pl
from jax.experimental.pallas import tpu as pltpu
from jax.sharding import PartitionSpec as P

TILE = 128
STEPS = 8
CBLK = 64
PBLK = 96
ORDER = TILE * STEPS

SWAP = [(0, 1), (1, 0)]
GROUP = ("sub", "y")
COL = ("xlo", "z")
VMEM = pl.BlockSpec(memory_space=pltpu.VMEM)
SMEM = pl.BlockSpec(memory_space=pltpu.SMEM)
ANY = pl.BlockSpec(memory_space=pl.ANY)
HBM = pl.BlockSpec(memory_space=pltpu.HBM)


def split(x):
    high = x.astype(jnp.bfloat16)
    return high, (x - high.astype(jnp.float32)).astype(jnp.bfloat16)


def dot3(a, b, contract):
    dot = functools.partial(
        lax.dot_general, dimension_numbers=(contract, ((), ())), preferred_element_type=jnp.float32
    )
    return dot(a[0], b[0]) + (dot(a[0], b[1]) + dot(a[1], b[0]))


def factor_tile(s_ref, x_ref, beside):
    full = (8, TILE)
    count = TILE // 8
    lane = lax.broadcasted_iota(jnp.int32, full, 1)
    sub = lax.broadcasted_iota(jnp.int32, full, 0)
    s = [s_ref[8 * i : 8 * i + 8, :] for i in range(count)]
    for p in range(count):
        j0 = 8 * p
        inside = (lane >= j0) & (lane < j0 + 8)
        panel = s[p]
        if p == 0:
            cols = [jnp.broadcast_to(panel[:, j0 + k : j0 + k + 1], full) for k in range(8)]
        c = [[jnp.broadcast_to(cols[m][k : k + 1, :], full) if m >= k else None for m in range(8)] for k in range(8)]
        e = []
        for k in range(8):
            row = jnp.broadcast_to(panel[k : k + 1, :], full)
            e.append(jnp.where(inside, jnp.where(lane == j0 + k, 1.0, 0.0), row))
        more = p + 1 < count
        if more:
            f = [jnp.broadcast_to(s[p + 1][:, j0 + k : j0 + k + 1], full) for k in range(8)]
            later = jnp.where(inside, 0.0, s[p + 1])
            cols = [jnp.broadcast_to(s[p + 1][:, j0 + 8 + k : j0 + 9 + k], full) for k in range(8)]
        root = [None] * 8
        for k in range(8):
            root[k] = lax.rsqrt(c[k][k])
            for m in range(k, 8):
                c[k][m] = c[k][m] * root[k]
            e[k] = e[k] * root[k]
            if more:
                f[k] = f[k] * root[k]
                later = later - f[k] * e[k]
                for n in range(8):
                    cols[n] = cols[n] - f[k] * jnp.broadcast_to(f[k][n : n + 1, :], full)
            for m in range(k + 1, 8):
                for n in range(m, 8):
                    c[m][n] = c[m][n] - c[k][m] * c[k][n]
                e[m] = e[m] - c[k][m] * e[k]
                if more:
                    f[m] = f[m] - c[k][m] * f[k]
        beside(p)
        if p + 2 < count:
            q = [None] * 8
            for k in reversed(range(8)):
                row = e[k]
                for m in range(k + 1, 8):
                    row = row - c[k][m] * q[m]
                q[k] = row * root[k]
            for i in range(p + 2, count):
                new = jnp.where(inside, 0.0, s[i])
                for k in range(8):
                    new = new - jnp.broadcast_to(s[i][:, j0 + k : j0 + k + 1], full) * q[k]
                s[i] = new
        if more:
            s[p + 1] = later
        out = jnp.zeros(full, jnp.float32)
        for k in range(8):
            out = jnp.where(sub == k, e[k], out)
        x_ref[j0 : j0 + 8, :] = jnp.where(lane < j0 + 8, out, 0.0)


def factor_kernel(
    where_ref, own_ref, other_ref, high_out, rest_out, lower_ref, w_ref, u_ref, s_ref, xn_ref, xk_ref, last_ref, high_ref, rest_ref,
    x_high_ref, x_rest_ref, sems
):
    core, tile_row, tile_col = where_ref[0], where_ref[1], where_ref[2]
    groups, depth = own_ref.shape[0], own_ref.shape[2]
    pitch = ORDER // groups
    for ref, which in ((own_ref, core), (other_ref, 1 - core)):
        for g in range(groups):
            begin = pl.multiple_of(g * pitch + which * depth, depth)
            for c in range(STEPS):
                w_ref[pl.ds(begin, depth), c * TILE : (c + 1) * TILE] = ref[g, c]
    block = lax.broadcasted_iota(jnp.int32, (TILE, ORDER), 1) // TILE

    def place(k):
        return pl.ds(pl.multiple_of(k * TILE, TILE), TILE)

    def finish(k):
        row = dot3(split(xk_ref[...]), split(w_ref[place(k), :]), ((1,), (0,)))
        u_ref[place(k), :] = row
        last_ref[...] = row
        last_ref[:, place(k)] = xk_ref[...]
        row = last_ref[...]
        x_high_ref[place(k), :], x_rest_ref[place(k), :] = split(jnp.where(block <= k, row, 0.0))
        high_ref[...], rest_ref[...] = split(row)

    def leave(k):
        pairs = ((x_high_ref, high_out), (x_rest_ref, rest_out))
        return [
            pltpu.make_async_copy(source.at[place(k)], target.at[place(k)], sems.at[i, k])
            for i, (source, target) in enumerate(pairs)
        ]

    def step(k, carry):
        before = k - 1

        def beside(p):
            if p == 0:
                finish(jnp.maximum(before, 0))
            elif p % 2 == 0:
                i = p // 2
                at = slice(i * TILE, (i + 1) * TILE)
                mine = jnp.where(i > before, last_ref[:, at], 0.0).T
                held = w_ref[at, :]
                held = jnp.where((block == before) & (i > before), 0.0, held)
                w_ref[at, :] = held - dot3(split(mine), (high_ref[...], rest_ref[...]), ((1,), (0,)))

        factor_tile(s_ref, xn_ref, beside)
        xk_ref[...] = xn_ref[...]
        after_k = jnp.minimum(k + 1, STEPS - 1)
        high, rest = split(dot3(split(xn_ref[...]), split(w_ref[place(k), place(after_k)]), ((1,), (0,))))
        s_ref[...] = w_ref[place(after_k), place(after_k)] - dot3((high.T, rest.T), (high, rest), ((1,), (0,)))

        @pl.when(k > 0)
        def _():
            for copy in leave(k - 1):
                copy.start()

        return carry

    xk_ref[...] = jnp.zeros((TILE, TILE), jnp.float32)
    s_ref[...] = w_ref[:TILE, :TILE]
    lax.fori_loop(0, STEPS, step, 0)
    finish(STEPS - 1)
    for copy in leave(STEPS - 1):
        copy.start()
    order = tile_row * TILE + lax.broadcasted_iota(jnp.int32, (TILE, TILE), 1)
    upper = tile_col * TILE + lax.broadcasted_iota(jnp.int32, (TILE, TILE), 0) <= order
    lower_ref[...] = jnp.where(upper, u_ref[place(tile_col), place(tile_row)], 0.0).T
    for k in range(STEPS):
        for copy in leave(k):
            copy.wait()


def factor(where, own, other):
    return pl.pallas_call(
        factor_kernel,
        out_shape=(
            jax.ShapeDtypeStruct((ORDER, ORDER), jnp.bfloat16),
            jax.ShapeDtypeStruct((ORDER, ORDER), jnp.bfloat16),
            jax.ShapeDtypeStruct((TILE, TILE), jnp.float32),
        ),
        in_specs=[SMEM, VMEM, VMEM],
        out_specs=(HBM, HBM, VMEM),
        scratch_shapes=[pltpu.VMEM((ORDER, ORDER), jnp.float32)] * 2
        + [pltpu.VMEM((TILE, TILE), jnp.float32)] * 3
        + [pltpu.VMEM((TILE, ORDER), jnp.float32)]
        + [pltpu.VMEM((TILE, ORDER), jnp.bfloat16)] * 2
        + [pltpu.VMEM((ORDER, ORDER), jnp.bfloat16)] * 2
        + [pltpu.SemaphoreType.DMA((2, STEPS))],
        compiler_params=pltpu.CompilerParams(vmem_limit_bytes=60 << 20),
        cost_estimate=pl.CostEstimate(flops=20_000_000_000, bytes_accessed=16 << 20, transcendentals=0),
        name="factor",
    )(where, own, other)


def chunks(width):
    wide = 2 * TILE
    return [(begin, min(wide, width - begin)) for begin in range(0, width, wide)]


def fetch(pairs, sems):
    copies = [pltpu.make_async_copy(source, target, sems.at[i]) for i, (source, target) in enumerate(pairs)]
    for copy in copies:
        copy.start()
    return copies


def solve_panels(col, copies, cols_in, rows_in, factor_ref, top, xs, cs, rs, ls, ts):
    wide = 2 * TILE
    copies[0].wait()
    copies[1].wait()
    copies[2].wait()
    for c in range(STEPS):
        at = slice(c * TILE, (c + 1) * TILE)
        cs[0][:, at], cs[1][:, at] = split(cols_in[c])
    for k in range(STEPS // 2):
        depth = wide * (k + 1)
        at = slice(k * wide, depth)
        x_now = (xs[0][at, :depth], xs[1][at, :depth])
        left = dot3((cs[0][:, :depth], cs[1][:, :depth]), x_now, ((1,), (1,)))
        ls[0][:, at], ls[1][:, at] = split(left)

    mine = pl.ds(pl.multiple_of(col * TILE, TILE), TILE)
    factor_ref[top:, :] = ls[0][:, mine].astype(jnp.float32) + ls[1][:, mine].astype(jnp.float32)
    copies[3].wait()
    if len(rows_in.shape) == 2:
        rs[0][...], rs[1][...] = split(rows_in[...])
    else:
        for i in range(STEPS):
            for j in range(2):
                begin = (j * STEPS // 2 + i // 2) * TILE + i % 2 * (TILE // 2)
                at = slice(begin, begin + TILE // 2)
                rs[0][at, :], rs[1][at, :] = split(rows_in[i, j])
    for k in range(STEPS // 2):
        depth = wide * (k + 1)
        at = slice(k * wide, depth)
        x_now = (xs[0][at, :depth], xs[1][at, :depth])
        for begin, width in chunks(rows_in.shape[-1]):
            here = slice(begin, begin + width)
            right = dot3(x_now, (rs[0][:depth, here], rs[1][:depth, here]), ((1,), (0,)))
            ts[0][at, here], ts[1][at, here] = split(right)


def child_kernel(where_ref, front_ref, cols_ref, rows_ref, x_high_ref, x_rest_ref, lower_ref, box_ref, factor_ref, *scratch):
    cols_in, rows_in, front_in, sems = scratch[:4]
    xs, cs, rs, ls, ts = (scratch[i : i + 2] for i in range(4, 14, 2))
    copies = fetch(
        [(x_high_ref, xs[0]), (x_rest_ref, xs[1]), (cols_ref, cols_in), (rows_ref, rows_in), (front_ref.at[TILE:, TILE:], front_in)], sems
    )
    solve_panels(where_ref[0], copies, cols_in, rows_in, factor_ref, TILE, xs, cs, rs, ls, ts)
    factor_ref[:TILE, :] = lower_ref[...]
    copies[4].wait()
    for begin, width in chunks(front_in.shape[1]):
        here = slice(begin, begin + width)
        left = (ls[0][...], ls[1][...])
        schur = front_in[:, here] - dot3(left, (ts[0][:, here], ts[1][:, here]), ((1,), (0,)))
        for b in range(begin // TILE, (begin + width) // TILE):
            at = slice(b * TILE - begin, (b + 1) * TILE - begin)
            for a in range(STEPS - 1):
                slot = where_ref[1 + a] * STEPS + where_ref[STEPS + b]
                box_ref[slot] = schur[a * TILE : (a + 1) * TILE, at]


def panel_scratch(rows, cols, gathered):
    given = [(STEPS, rows, TILE), gathered, (rows, cols)]
    pairs = [(ORDER, ORDER), (rows, ORDER), (ORDER, cols), (rows, ORDER), (ORDER, cols)]
    return (
        [pltpu.VMEM(shape, jnp.float32) for shape in given]
        + [pltpu.SemaphoreType.DMA((5,))]
        + [pltpu.VMEM(shape, jnp.bfloat16) for shape in pairs for _ in range(2)]
    )


def child_update(where, front, cols, rows, x, lower):
    kept = front.shape[0] - TILE, front.shape[1] - TILE
    return pl.pallas_call(
        child_kernel,
        out_shape=(
            jax.ShapeDtypeStruct((STEPS * STEPS, TILE, TILE), jnp.float32),
            jax.ShapeDtypeStruct((front.shape[0], TILE), jnp.float32),
        ),
        in_specs=[SMEM] + [ANY] * 5 + [VMEM],
        out_specs=(VMEM, VMEM),
        scratch_shapes=panel_scratch(*kept, rows.shape),
        compiler_params=pltpu.CompilerParams(vmem_limit_bytes=58 << 20),
        name="child_update",
    )(where, front, cols, rows, *x, lower)


def parent_kernel(where_ref, front_ref, cols_ref, rows_ref, x_high_ref, x_rest_ref, lower_ref, out_ref, factor_ref, *scratch):
    cols_in, rows_in, front_in, sems = scratch[:4]
    xs, cs, rs, ls, ts = (scratch[i : i + 2] for i in range(4, 14, 2))
    col, core = where_ref[0], where_ref[1]
    copies = fetch([(x_high_ref, xs[0]), (x_rest_ref, xs[1]), (cols_ref, cols_in), (rows_ref, rows_in), (front_ref.at[:, TILE:], front_in)], sems)
    solve_panels(col, copies, cols_in, rows_in, factor_ref, 0, xs, cs, rs, ls, ts)

    @pl.when(core == 0)
    def _():
        factor_ref[:TILE, :] = lower_ref[...]

    copies[4].wait()
    out_ref[:, :TILE] = jnp.zeros((front_in.shape[0], TILE), jnp.float32)
    for begin, width in chunks(front_in.shape[1]):
        here = slice(begin, begin + width)
        left = (ls[0][...], ls[1][...])
        out_ref[:, TILE + begin : TILE + begin + width] = front_in[:, here] - dot3(
            left, (ts[0][:, here], ts[1][:, here]), ((1,), (0,))
        )

    @pl.when(core == 0)
    def _():
        out_ref[:TILE, :] = jnp.zeros((TILE, out_ref.shape[1]), jnp.float32)


def parent_update(where, front, cols, rows, x, lower):
    return pl.pallas_call(
        parent_kernel,
        out_shape=(
            jax.ShapeDtypeStruct(front.shape, jnp.float32),
            jax.ShapeDtypeStruct((front.shape[0], TILE), jnp.float32),
        ),
        in_specs=[SMEM] + [ANY] * 5 + [VMEM],
        out_specs=(VMEM, VMEM),
        scratch_shapes=panel_scratch(front.shape[0], front.shape[1] - TILE, rows.shape),
        compiler_params=pltpu.CompilerParams(vmem_limit_bytes=60 << 20),
        name="parent_update",
    )(where, front, cols, rows, *x, lower)


def assemble_kernel(rows_ref, cols_ref, front_ref, own_ref, other_ref, result_ref, out_ref, sems):
    tiles_row, tiles_col = (n // TILE for n in front_ref.shape)
    out_ref[...] = front_ref[...]
    def add_row(child, i, at):
        source = rows_ref[child * tiles_row + i]

        def add(box_ref, base):
            for j in range(tiles_col):
                place = cols_ref[child * tiles_col + j]

                @pl.when(place >= 0)
                def _():
                    out_ref[at, j * TILE : (j + 1) * TILE] += box_ref[base + place]

        @pl.when((source >= 0) & (source < STEPS * STEPS))
        def _():
            add(own_ref, source)

        @pl.when(source >= STEPS * STEPS)
        def _():
            add(other_ref, source - STEPS * STEPS)

    copies = []
    for i in range(tiles_row):
        at = slice(i * TILE, (i + 1) * TILE)
        for child in range(2):
            add_row(child, i, at)
        copies.append(pltpu.make_async_copy(out_ref.at[at], result_ref.at[at], sems.at[i]))
        copies[-1].start()
    for copy in copies:
        copy.wait()


def assemble(rows, cols, front, own, other):
    return pl.pallas_call(
        assemble_kernel,
        out_shape=jax.ShapeDtypeStruct(front.shape, jnp.float32),
        in_specs=[SMEM, SMEM] + [VMEM] * 3,
        out_specs=HBM,
        scratch_shapes=[pltpu.VMEM(front.shape, jnp.float32), pltpu.SemaphoreType.DMA((front.shape[0] // TILE,))],
        compiler_params=pltpu.CompilerParams(vmem_limit_bytes=60 << 20),
        name="assemble",
    )(rows, cols, front, own, other)


def spread(x, axes, first=None):
    count = lax.axis_size(axes)
    copies = jnp.broadcast_to(x[None], (count,) + x.shape)
    if first is not None:
        copies = after(copies, first)
    return lax.all_to_all(copies, axes, 0, 0, tiled=True)


def after(x, first):
    return lax.optimization_barrier((x, first))[0]


def local(child_fronts, child_map, parent_front):
    child = lax.axis_index("sub")
    core = lax.axis_index("core")
    row = lax.axis_index(("y", "core"))
    col = lax.axis_index(COL)
    group = lax.axis_index(GROUP)
    front = child_fronts[0]
    kept = CBLK // STEPS - 1

    own = spread(front[:TILE, :TILE], ("y",) + COL).reshape(-1, STEPS, TILE, TILE)
    rows = lax.all_gather(after(front[:TILE, TILE:], own), ("y", "core"), axis=0, tiled=True)
    other = lax.ppermute(own, "core", SWAP)
    columns = spread(front[TILE:, :TILE], COL, own)
    *inverse, lower = factor(jnp.stack([core, row, col]).astype(jnp.int32), own, other)
    columns = after(columns, lower)
    mine = child_map[child] // (PBLK // STEPS)
    where = jnp.concatenate(
        [
            col.reshape(1),
            lax.dynamic_slice(mine, (row * kept,), (kept,)),
            lax.dynamic_slice(mine, (col * kept,), (kept,)),
        ]
    ).astype(jnp.int32)
    box, child_factor = child_update(where, front, columns, rows, inverse, lower)

    box = lax.all_to_all(box, GROUP + COL, 0, 0, tiled=True)
    box_other = lax.ppermute(box, "core", SWAP)
    tiles_row, tiles_col = parent_front.shape[0] // TILE, parent_front.shape[1] // TILE
    blocks = jnp.arange(PBLK, dtype=jnp.int32)
    number = jnp.arange(CBLK - STEPS, dtype=jnp.int32)
    source = jnp.max(jnp.where(child_map[:, :, None] == blocks, number[:, None], -1), axis=1)
    source_row = lax.dynamic_slice(source, (0, (2 * group + core) * tiles_row), (2, tiles_row))
    source_col = lax.dynamic_slice(source, (0, col * tiles_col), (2, tiles_col))
    whose = (source_row // kept % 2 != core).astype(jnp.int32) * (STEPS * STEPS)
    place = whose + jnp.arange(2, dtype=jnp.int32)[:, None] * (STEPS * STEPS // 2) + source_row // (2 * kept) * STEPS
    place_row = jnp.where(source_row >= 0, place, -1)
    place_col = jnp.where(source_col >= 0, source_col // kept, -1)
    front = assemble(place_row.reshape(-1), place_col.reshape(-1), parent_front, box, box_other)

    down = [(0, 1)]
    half = TILE // 2
    strip = jnp.where(core == 0, front[:half, :], lax.ppermute(front[half:TILE, :], "core", down))
    strip_other = lax.ppermute(strip[:, TILE:], "sub", SWAP)
    own = spread(strip[:, :TILE], GROUP + COL).reshape(-1, STEPS, half, TILE)
    other = lax.ppermute(own, "core", SWAP)
    strip_other = after(strip_other, own)
    both = jnp.stack([jnp.where(child == i, strip[:, TILE:], strip_other) for i in range(2)])
    rows = lax.all_gather(both, ("y", "core"), axis=0)
    columns = spread(front[:, :TILE], COL, own)
    *inverse, lower = factor(jnp.stack([core, group, col]).astype(jnp.int32), own, other)
    rows, columns = after((rows, columns), lower)
    where = jnp.stack([col, core]).astype(jnp.int32)
    update, parent_factor = parent_update(where, front, columns, rows, inverse, lower)
    return (child_factor[None], parent_factor, update)


def solution(mesh):
    shape = (2, 4, 2, 2, 4)
    fine = jax.sharding.Mesh(mesh.devices.reshape(shape), ("sub", "y", "core", "xlo", "z"))
    in_specs = (P("sub", ("y", "core"), COL), P(), P(("sub", "y", "core"), COL))
    out_specs = (P("sub", ("y", "core"), COL), P(("sub", "y", "core"), COL), P(("sub", "y", "core"), COL))
    return jax.shard_map(local, mesh=fine, in_specs=in_specs, out_specs=out_specs, check_vma=False)
```

profile of v0, /device:TPU:1, one launch (start us, length us, event | category | flops | bytes accessed | tf_op | source)
XLA Modules:
  0.0 326.5 jit_solution(15583738481096772565)
XLA Ops:
  7.2 0.8 slice.35
  8.0 1.6 broadcast_in_dim.27
  9.6 9.8 %all-to-all-start = ((f32[32,128,128]{2,1,0:T(8,128)}), f32[32,128,128]{2,1,0:T(8,128)S(1)}, u32[]{:S(2)}, u32[]{:S(2)}) async-start(f32[32,128,128]{2,1,0:T(8,128)} %broadcast_in_dim.27), calls=%async_computation | async-start | bytes 4194304 | tf_op jit(solution)/shard_map/all_to_all | solution.py:377
  19.4 1.8 slice.36
  21.3 26.2 %all-to-all-done = f32[32,128,128]{2,1,0:T(8,128)S(1)} async-done(((f32[32,128,128]{2,1,0:T(8,128)}), f32[32,128,128]{2,1,0:T(8,128)S(1)}, u32[]{:S(2)}, u32[]{:S(2)}) %all-to-all-start) | async-done | bytes 2097184 | tf_op jit(solution)/shard_map/all_to_all | solution.py:377
  47.5 2.2 collective-permute-start
  49.7 1.0 slice.34
  50.7 2.1 broadcast_in_dim.26
  52.8 4.7 %all-to-all-start.1 = ((f32[8,896,128]{2,1,0:T(8,128)}), f32[8,896,128]{2,1,0:T(8,128)}, u32[]{:S(2)}, u32[]{:S(2)}) async-start(f32[8,896,128]{2,1,0:T(8,128)} %broadcast_in_dim.26), calls=%async_computation.1 | async-start | bytes 7340032 | tf_op jit(solution)/shard_map/all_to_all | solution.py:377
  58.8 37.6 %factor.2 = (bf16[1024,1024]{1,0:T(8,128)(2,1)}, bf16[1024,1024]{1,0:T(8,128)(2,1)}, f32[128,128]{1,0:T(8,128)}) custom-call(s32[3]{0:T(128)} %add_add_fusion.where_ref, f32[4,8,128,128]{3,2,1,0:T(8,128)} %bitcast.23, f32[4,8,128,128]{3,2,1,0:T(8,128)} %collective-permute-done.other_ref), custom_call_target="tpu_custom_call" | custom-call | flops 20000000000 | bytes 16777216 | tf_op jit(solution)/shard_map/factor/pallas_call | solution.py:172
  96.4 4.2 %all-to-all-done.1.cols_ref = f32[8,896,128]{2,1,0:T(8,128)} async-done(((f32[8,896,128]{2,1,0:T(8,128)}), f32[8,896,128]{2,1,0:T(8,128)}, u32[]{:S(2)}, u32[]{:S(2)}) %all-to-all-start.1) | async-done | bytes 3670048 | tf_op jit(solution)/shard_map/all_to_all | solution.py:377
  100.5 21.9 %child_update.1 = (f32[64,128,128]{2,1,0:T(8,128)}, f32[1024,128]{1,0:T(8,128)}) custom-call(s32[15]{0:T(128)} %pad_add_fusion.where_ref, f32[1024,1024]{1,0:T(8,128)} %bitcast.20, f32[8,896,128]{2,1,0:T(8,128)} %all-to-all-done.1.cols_ref, f32[1024,896]{1,0:T(8,128)} %all-gather.4.cloned.1.call-done.rows_ref, ...), custom_call_target="tpu_custom_call" | custom-call | tf_op jit(solution)/shard_map/child_update/pallas_call | solution.py:273
  122.5 58.2 %all_to_all.25.own_ref = f32[64,128,128]{2,1,0:T(8,128)} all-to-all(f32[64,128,128]{2,1,0:T(8,128)} %get-tuple-element.27), channel_id=1, replica_groups=mesh['sub'=2,'y'=4,'core'=2,'xlo'=2,'z'=4] {'sub','y','xlo','z'}, dimensions={0} | all-to-all | bytes 8388608 | tf_op jit(solution)/shard_map/all_to_all | solution.py:409
  180.6 2.7 collective-permute-start.1
  183.5 0.7 reshape.44.cols_ref
  184.9 5.6 %collective-permute-done.1.other_ref = f32[64,128,128]{2,1,0:T(8,128)} collective-permute-done((f32[64,128,128]{2,1,0:T(8,128)}, f32[64,128,128]{2,1,0:T(8,128)}, u32[]{:S(2)}, u32[]{:S(2)}) %collective-permute-start.1) | collective-permute-done | bytes 4194336 | tf_op jit(solution)/shard_map/ppermute | solution.py:410
  190.4 7.4 %assemble.1.front_ref = f32[768,1536]{1,0:T(8,128)} custom-call(s32[12]{0:T(128)} %reshape.43.rows_ref, s32[24]{0:T(128)} %reshape.44.cols_ref, f32[768,1536]{1,0:T(8,128)} %front_ref.1, f32[64,128,128]{2,1,0:T(8,128)} %all_to_all.25.own_ref, f32[64,128,128]{2,1,0:T(8,128)} %collective-permute-done.1.other_ref), custom_call_target="tpu_custom_call" | custom-call | tf_op jit(solution)/shard_map/assemble/pallas_call | solution.py:361
  197.9 1.0 slice.38
  198.9 1.3 collective-permute-start.2
  200.2 2.3 collective-permute-done.2
  202.5 1.0 slice_select_fusion
  203.6 1.6 broadcast_in_dim.31
  205.2 7.3 %all-to-all-start.3 = ((f32[64,64,128]{2,1,0:T(8,128)}), f32[64,64,128]{2,1,0:T(8,128)}, u32[]{:S(2)}, u32[]{:S(2)}) async-start(f32[64,64,128]{2,1,0:T(8,128)} %broadcast_in_dim.31), calls=%async_computation.3 | async-start | bytes 4194304 | tf_op jit(solution)/shard_map/all_to_all | solution.py:377
  212.5 2.6 collective-permute-start.3
  215.2 30.0 %collective-permute-done.3 = f32[64,1408]{1,0:T(8,128)S(1)} collective-permute-done((f32[64,1408]{1,0:T(8,128)S(1)}, f32[64,1408]{1,0:T(8,128)S(1)}, u32[]{:S(2)}, u32[]{:S(2)}) %collective-permute-start.3) | collective-permute-done | bytes 360480 | tf_op jit(solution)/shard_map/ppermute | solution.py:426
  245.3 0.9 pad_maximum_fusion
  246.2 1.4 collective-permute-start.4
  247.6 1.9 broadcast_in_dim.32
  249.4 4.0 %all-to-all-start.4 = ((f32[8,768,128]{2,1,0:T(8,128)}), f32[8,768,128]{2,1,0:T(8,128)S(1)}, u32[]{:S(2)}, u32[]{:S(2)}) async-start(f32[8,768,128]{2,1,0:T(8,128)} %broadcast_in_dim.32), calls=%async_computation.4 | async-start | bytes 6291456 | tf_op jit(solution)/shard_map/all_to_all | solution.py:377
  254.7 38.0 %factor.3 = (bf16[1024,1024]{1,0:T(8,128)(2,1)}, bf16[1024,1024]{1,0:T(8,128)(2,1)}, f32[128,128]{1,0:T(8,128)}) custom-call(s32[3]{0:T(128)} %add_add_fusion.1.where_ref, f32[8,8,64,128]{3,2,1,0:T(8,128)} %bitcast.8.own_ref, f32[8,8,64,128]{3,2,1,0:T(8,128)} %collective-permute-done.4.other_ref), custom_call_target="tpu_custom_call" | custom-call | flops 20000000000 | bytes 16777216 | tf_op jit(solution)/shard_map/factor/pallas_call | solution.py:172
  292.7 1.7 copy-done
  294.5 24.9 %parent_update.1 = (f32[768,1536]{1,0:T(8,128)}, f32[768,128]{1,0:T(8,128)}) custom-call(s32[2]{0:T(128)} %pad_add_fusion.1.where_ref, f32[768,1536]{1,0:T(8,128)} %assemble.1.front_ref, f32[8,768,128]{2,1,0:T(8,128)} %copy-done, f32[8,2,64,1408]{3,2,1,0:T(8,128)} %bitcast.21, bf16[1024,1024]{1,0:T(8,128)(2,1)} %get-tuple-element.33.x_high_ref, ...), custom_call_target="tpu_custom_call" | custom-call | tf_op jit(solution)/shard_map/parent_update/pallas_call | solution.py:313
  (31 shorter events, 3.7 us)
Async XLA Ops:
  9.6 37.9 %all-to-all-start = ((f32[32,128,128]{2,1,0:T(8,128)}), f32[32,128,128]{2,1,0:T(8,128)S(1)}, u32[]{:S(2)}, u32[]{:S(2)}) async-start(f32[32,128,128]{2,1,0:T(8,128)} %broadcast_in_dim.27), calls=%async_computation | async-start | bytes 4194304 | tf_op jit(solution)/shard_map/all_to_all | solution.py:377
  19.4 81.2 %all-gather.4.cloned.1.call-start = ((), (), s32[]{:S(2)}) async-start(), calls=%async_computation.5 | async-start | bytes 4128768 | tf_op jit(solution)/shard_map/all_gather | solution.py:394
  47.4 5.4 %copy-start.1 = (f32[32,128,128]{2,1,0:T(8,128)}, f32[32,128,128]{2,1,0:T(8,128)S(1)}, u32[]{:S(2)}) copy-start(f32[32,128,128]{2,1,0:T(8,128)S(1)} %all-to-all-done) | copy-start | bytes 6291460
  47.5 11.3 %collective-permute-start = (f32[4,8,128,128]{3,2,1,0:T(8,128)S(1)}, f32[4,8,128,128]{3,2,1,0:T(8,128)}, u32[]{:S(2)}, u32[]{:S(2)}) collective-permute-start(f32[4,8,128,128]{3,2,1,0:T(8,128)S(1)} %bitcast.22), channel_id=1, source_target_pairs={{0,8},{8,0},{1,9},{9,1},{2,10},{10,2},{3,11},{11,3},{4,12},{12,4},... | collective-permute-start | bytes 6291464 | tf_op jit(solution)/shard_map/ppermute | solution.py:395
  52.8 4.7 %copy-start.2 = (s32[2,56]{1,0:T(2,128)S(1)}, s32[2,56]{1,0:T(2,128)}, u32[]{:S(2)}) copy-start(s32[2,56]{1,0:T(2,128)} %param.4) | copy-start | bytes 1348
  52.8 47.7 %all-to-all-start.1 = ((f32[8,896,128]{2,1,0:T(8,128)}), f32[8,896,128]{2,1,0:T(8,128)}, u32[]{:S(2)}, u32[]{:S(2)}) async-start(f32[8,896,128]{2,1,0:T(8,128)} %broadcast_in_dim.26), calls=%async_computation.1 | async-start | bytes 7340032 | tf_op jit(solution)/shard_map/all_to_all | solution.py:377
  180.6 9.8 %collective-permute-start.1 = (f32[64,128,128]{2,1,0:T(8,128)}, f32[64,128,128]{2,1,0:T(8,128)}, u32[]{:S(2)}, u32[]{:S(2)}) collective-permute-start(f32[64,128,128]{2,1,0:T(8,128)} %all_to_all.25.own_ref), channel_id=1, source_target_pairs={{0,8},{8,0},{1,9},{9,1},{2,10},{10,2},{3,11},{11,3},{4,12},{12,4},... | collective-permute-start | bytes 12582920 | tf_op jit(solution)/shard_map/ppermute | solution.py:410
  198.9 3.6 %collective-permute-start.2 = (f32[64,1536]{1,0:T(8,128)S(1)}, f32[64,1536]{1,0:T(8,128)S(1)}, u32[]{:S(2)}, u32[]{:S(2)}) collective-permute-start(f32[64,1536]{1,0:T(8,128)S(1)} %slice.38), channel_id=1, source_target_pairs={{0,8},{1,9},{2,10},{3,11},{4,12},{5,13},{6,14},{7,15},{16,24},{17,... | collective-permute-start | bytes 1179656 | tf_op jit(solution)/shard_map/ppermute | solution.py:425
  205.2 42.4 %slice-start = ((f32[768,1536]{1,0:T(8,128)}), f32[768,128]{1,0:T(8,128)S(1)}, s32[]{:S(2)}) async-start(f32[768,1536]{1,0:T(8,128)} %assemble.1.front_ref), calls=%async_computation.7 | async-start | bytes 786432 | tf_op jit(solution)/shard_map/slice | solution.py:432
  205.2 40.1 %all-to-all-start.3 = ((f32[64,64,128]{2,1,0:T(8,128)}), f32[64,64,128]{2,1,0:T(8,128)}, u32[]{:S(2)}, u32[]{:S(2)}) async-start(f32[64,64,128]{2,1,0:T(8,128)} %broadcast_in_dim.31), calls=%async_computation.3 | async-start | bytes 4194304 | tf_op jit(solution)/shard_map/all_to_all | solution.py:377
  212.5 80.3 %all-gather.6.cloned.1.call-start = ((), (), s32[]{:S(2)}) async-start(), calls=%async_computation.6 | async-start | bytes 6488064 | tf_op jit(solution)/shard_map/all_gather | solution.py:431
  212.5 32.7 %collective-permute-start.3 = (f32[64,1408]{1,0:T(8,128)S(1)}, f32[64,1408]{1,0:T(8,128)S(1)}, u32[]{:S(2)}, u32[]{:S(2)}) collective-permute-start(f32[64,1408]{1,0:T(8,128)S(1)} %slice.39), channel_id=1, source_target_pairs={{0,64},{64,0},{1,65},{65,1},{2,66},{66,2},{3,67},{67,3},{4,68},{68... | collective-permute-start | bytes 1081352 | tf_op jit(solution)/shard_map/ppermute | solution.py:426
  246.2 8.5 %collective-permute-start.4 = (f32[8,8,64,128]{3,2,1,0:T(8,128)}, f32[8,8,64,128]{3,2,1,0:T(8,128)}, u32[]{:S(2)}, u32[]{:S(2)}) collective-permute-start(f32[8,8,64,128]{3,2,1,0:T(8,128)} %bitcast.8.own_ref), channel_id=1, source_target_pairs={{0,8},{8,0},{1,9},{9,1},{2,10},{10,2},{3,11},{11,3},{4,12},{12,4},... | collective-permute-start | bytes 6291464 | tf_op jit(solution)/shard_map/ppermute | solution.py:428
  249.4 43.3 %all-to-all-start.4 = ((f32[8,768,128]{2,1,0:T(8,128)}), f32[8,768,128]{2,1,0:T(8,128)S(1)}, u32[]{:S(2)}, u32[]{:S(2)}) async-start(f32[8,768,128]{2,1,0:T(8,128)} %broadcast_in_dim.32), calls=%async_computation.4 | async-start | bytes 6291456 | tf_op jit(solution)/shard_map/all_to_all | solution.py:377
  292.7 1.8 copy-start
Sparse Core Ops, SparseCore 0:
  47.6 29.5 all-gather.3
  246.3 39.3 all-gather.5
where the time goes:
time: 332 us; the launch traced here: 326 us
  Pallas kernels  130 us (39%)
  waiting for transfers between devices  68.3 us (21%)
  blocking collectives  58.2 us (18%)
  starting transfers between devices  36 us (11%)
  local copies, waits for them, and re-layouts  14.9 us (4%)
  between operations  14.4 us (4%)
  other arithmetic  4.75 us (1%)
    pallas_call x2, Pallas kernels, factor(): pl.pallas_call(factor_kernel, out_shape=(jax.ShapeDtypeStruct((ORDER, ORD...  75.6 us
    all_to_all x1, blocking collectives, local(): box = lax.all_to_all(box, GROUP + COL, 0, 0, tiled=True)  58.2 us
    all_to_all x4, waiting for transfers between devices, spread(): return lax.all_to_all(copies, axes, 0, 0, tiled=True)  30.3 us
    ppermute x1, waiting for transfers between devices, local(): strip_other = lax.ppermute(strip[:, TILE:], 'sub', SWAP)  30 us
    all_to_all x4, starting transfers between devices, spread(): return lax.all_to_all(copies, axes, 0, 0, tiled=True)  25.8 us
    pallas_call x1, Pallas kernels, parent_update(): pl.pallas_call(parent_kernel, out_shape=(jax.ShapeDtypeStruct(front.shape...  24.9 us
    pallas_call x1, Pallas kernels, child_update(): pl.pallas_call(child_kernel, out_shape=(jax.ShapeDtypeStruct((STEPS * STE...  21.9 us
    pallas_call x1, Pallas kernels, assemble(): pl.pallas_call(assemble_kernel, out_shape=jax.ShapeDtypeStruct(front.shap...  7.44 us
  transfers between devices with their start and end apart: 11, of which 5 were waited for; matrix products, arithmetic and copies ran while one was open for 3% of the time, Pallas kernels for 23%

commit v1 on v0

--- a/solution.py
+++ b/solution.py
@@ -94,18 +94,56 @@
         x_ref[j0 : j0 + 8, :] = jnp.where(lane < j0 + 8, out, 0.0)
 
 
+def pack(tile, row, col):
+    half = TILE // 2
+    at = lax.broadcasted_iota(jnp.int32, (half, half), 0) - lax.broadcasted_iota(jnp.int32, (half, half), 1)
+    corner = tile[half:, half:]
+    mixed = jnp.concatenate([jnp.where(at > 0, corner, tile[:half, :half]), tile[:half, half:]], 1)
+    body = jnp.where(row == col, mixed, jnp.where(row < col, tile[:half], tile[:, half:].T))
+    middle = jnp.sum(jnp.where(at == 0, corner, 0.0), axis=0, keepdims=True)
+    return jnp.concatenate([body, jnp.pad(middle, ((0, 15), (0, half)))], 0)
+
+
+def unpack(refs, w_ref):
+    half = TILE // 2
+    groups = refs[0].shape[0]
+    lane = lax.broadcasted_iota(jnp.int32, (TILE, TILE), 1)
+    sub = lax.broadcasted_iota(jnp.int32, (TILE, TILE), 0)
+    for r in range(STEPS):
+        for c in range(STEPS):
+            if groups < STEPS:
+                piece = refs[r % 2][r // 2, c]
+            else:
+                piece = jnp.concatenate([refs[0][r, c], refs[1][r, c]], 0)
+            body = piece[:half]
+            if r < c:
+                w_ref[r * TILE : r * TILE + half, c * TILE : (c + 1) * TILE] = body
+            elif r > c:
+                w_ref[c * TILE + half : (c + 1) * TILE, r * TILE : (r + 1) * TILE] = body
+            else:
+                turned = jnp.concatenate([body, jnp.zeros((half, TILE), jnp.float32)], 0).T[:half]
+                middle = jnp.broadcast_to(piece[half : half + 1], (half, TILE))
+                order = lane[:half] - sub[:half]
+                low = jnp.where(order == 0, middle, jnp.where(order > 0, turned, 0.0))
+                low = jnp.where(lane[:half] >= half, pltpu.roll(jnp.where(lane[:half] < half, low, 0.0), half, 1), 0.0)
+                whole = jnp.concatenate([body, low], 0)
+                w_ref[r * TILE : (r + 1) * TILE, r * TILE : (r + 1) * TILE] = jnp.where(lane >= sub, whole, whole.T)
+
+
 def factor_kernel(
     where_ref, own_ref, other_ref, high_out, rest_out, lower_ref, w_ref, u_ref, s_ref, xn_ref, xk_ref, last_ref, high_ref, rest_ref,
     x_high_ref, x_rest_ref, sems
 ):
     core, tile_row, tile_col = where_ref[0], where_ref[1], where_ref[2]
-    groups, depth = own_ref.shape[0], own_ref.shape[2]
-    pitch = ORDER // groups
-    for ref, which in ((own_ref, core), (other_ref, 1 - core)):
-        for g in range(groups):
-            begin = pl.multiple_of(g * pitch + which * depth, depth)
-            for c in range(STEPS):
-                w_ref[pl.ds(begin, depth), c * TILE : (c + 1) * TILE] = ref[g, c]
+
+    @pl.when(core == 0)
+    def _():
+        unpack((own_ref, other_ref), w_ref)
+
+    @pl.when(core == 1)
+    def _():
+        unpack((other_ref, own_ref), w_ref)
+
     block = lax.broadcasted_iota(jnp.int32, (TILE, ORDER), 1) // TILE
 
     def place(k):
@@ -390,7 +428,8 @@
     front = child_fronts[0]
     kept = CBLK // STEPS - 1
 
-    own = spread(front[:TILE, :TILE], ("y",) + COL).reshape(-1, STEPS, TILE, TILE)
+    piece = pack(front[:TILE, :TILE], row, col)[:72]
+    own = spread(piece, ("y",) + COL).reshape((-1, STEPS) + piece.shape)
     rows = lax.all_gather(after(front[:TILE, TILE:], own), ("y", "core"), axis=0, tiled=True)
     other = lax.ppermute(own, "core", SWAP)
     columns = spread(front[TILE:, :TILE], COL, own)
@@ -424,7 +463,10 @@
     half = TILE // 2
     strip = jnp.where(core == 0, front[:half, :], lax.ppermute(front[half:TILE, :], "core", down))
     strip_other = lax.ppermute(strip[:, TILE:], "sub", SWAP)
-    own = spread(strip[:, :TILE], GROUP + COL).reshape(-1, STEPS, half, TILE)
+    piece = pack(front[:TILE, :TILE], group, col)
+    part = piece.shape[0] // 2
+    piece = jnp.where(core == 0, piece[:part], lax.ppermute(piece[part:], "core", down))
+    own = spread(piece, GROUP + COL).reshape((-1, STEPS) + piece.shape)
     other = lax.ppermute(own, "core", SWAP)
     strip_other = after(strip_other, own)
     both = jnp.stack([jnp.where(child == i, strip[:, TILE:], strip_other) for i in range(2)])

time: 332 us -> 315 us (0.949)
  waiting for transfers between devices: 68.3 us -> 43.5 us
  local copies, waits for them, and re-layouts: 14.9 us -> 19.1 us
    all_to_all x4, waiting for transfers between devices: 30.3 us -> 15 us  [spread(): return lax.all_to_all(copies, axes, 0, 0, tiled=True)]
    ppermute x1, waiting for transfers between devices: 30 us -> 16.8 us  [local(): strip_other = lax.ppermute(strip[:, TILE:], 'sub', SWAP)]
  transfers between devices with their start and end apart: 11 -> 12, of which waited for: 5 -> 6; matrix products, arithmetic and copies ran while one was open for 3% -> 4% of each run, Pallas kernels for 23% -> 24%
where the time goes in v1:
time: 315 us; the launch traced here: 309 us
  Pallas kernels  130 us (41%)
  blocking collectives  59.4 us (19%)
  waiting for transfers between devices  43.5 us (14%)
  starting transfers between devices  36.5 us (12%)
  local copies, waits for them, and re-layouts  19.1 us (6%)
  between operations  14.5 us (5%)
  other arithmetic  6.06 us (2%)
    pallas_call x2, Pallas kernels, factor(): pl.pallas_call(factor_kernel, out_shape=(jax.ShapeDtypeStruct((ORDER, ORD...  75 us
    all_to_all x1, blocking collectives, local(): box = lax.all_to_all(box, GROUP + COL, 0, 0, tiled=True)  59.4 us
    all_to_all x4, starting transfers between devices, spread(): return lax.all_to_all(copies, axes, 0, 0, tiled=True)  25.6 us
    pallas_call x1, Pallas kernels, parent_update(): pl.pallas_call(parent_kernel, out_shape=(jax.ShapeDtypeStruct(front.shape...  24.9 us
    pallas_call x1, Pallas kernels, child_update(): pl.pallas_call(child_kernel, out_shape=(jax.ShapeDtypeStruct((STEPS * STE...  21.9 us
    ppermute x1, waiting for transfers between devices, local(): strip_other = lax.ppermute(strip[:, TILE:], 'sub', SWAP)  16.8 us
    all_to_all x4, waiting for transfers between devices, spread(): return lax.all_to_all(copies, axes, 0, 0, tiled=True)  15 us
    pallas_call x1, Pallas kernels, assemble(): pl.pallas_call(assemble_kernel, out_shape=jax.ShapeDtypeStruct(front.shap...  7.8 us
  transfers between devices with their start and end apart: 12, of which 6 were waited for; matrix products, arithmetic and copies ran while one was open for 4% of the time, Pallas kernels for 24%

profile of v1, /device:TPU:1, one launch (start us, length us, event | category | flops | bytes accessed | tf_op | source)
XLA Modules:
  0.0 308.7 jit_solution(16129297114715667994)
XLA Ops:
  10.5 1.1 broadcast_in_dim.61
  11.6 9.8 %all-to-all-start = ((f32[32,72,128]{2,1,0:T(8,128)}), f32[32,72,128]{2,1,0:T(8,128)S(1)}, u32[]{:S(2)}, u32[]{:S(2)}) async-start(f32[32,72,128]{2,1,0:T(8,128)} %broadcast_in_dim.61), calls=%async_computation | async-start | bytes 2359296 | tf_op jit(solution)/shard_map/all_to_all | solution.py:415
  21.5 1.8 slice.96
  23.3 15.0 %all-to-all-done = f32[32,72,128]{2,1,0:T(8,128)S(1)} async-done(((f32[32,72,128]{2,1,0:T(8,128)}), f32[32,72,128]{2,1,0:T(8,128)S(1)}, u32[]{:S(2)}, u32[]{:S(2)}) %all-to-all-start) | async-done | bytes 1179680 | tf_op jit(solution)/shard_map/all_to_all | solution.py:415
  38.3 1.4 slice.90
  39.8 2.1 broadcast_in_dim.35
  41.8 4.7 %all-to-all-start.1 = ((f32[8,896,128]{2,1,0:T(8,128)}), f32[8,896,128]{2,1,0:T(8,128)}, u32[]{:S(2)}, u32[]{:S(2)}) async-start(f32[8,896,128]{2,1,0:T(8,128)} %broadcast_in_dim.35), calls=%async_computation.1 | async-start | bytes 7340032 | tf_op jit(solution)/shard_map/all_to_all | solution.py:415
  46.5 1.9 collective-permute-start
  49.8 1.8 collective-permute-done.other_ref
  51.6 1.0 copy-done.3
  52.6 37.3 %factor.2 = (bf16[1024,1024]{1,0:T(8,128)(2,1)}, bf16[1024,1024]{1,0:T(8,128)(2,1)}, f32[128,128]{1,0:T(8,128)}) custom-call(s32[3]{0:T(128)} %add_add_fusion.where_ref, f32[4,8,72,128]{3,2,1,0:T(8,128)} %bitcast.39, f32[4,8,72,128]{3,2,1,0:T(8,128)} %copy-done.3), custom_call_target="tpu_custom_call" | custom-call | flops 20000000000 | bytes 16777216 | tf_op jit(solution)/shard_map/factor/pallas_call | solution.py:210
  89.9 21.9 %child_update.1 = (f32[64,128,128]{2,1,0:T(8,128)}, f32[1024,128]{1,0:T(8,128)}) custom-call(s32[15]{0:T(128)} %pad_add_fusion.where_ref, f32[1024,1024]{1,0:T(8,128)} %bitcast.36, f32[8,896,128]{2,1,0:T(8,128)} %all-to-all-done.1.cols_ref, f32[1024,896]{1,0:T(8,128)} %all-gather.4.cloned.1.call-done.rows_ref, ...), custom_call_target="tpu_custom_call" | custom-call | tf_op jit(solution)/shard_map/child_update/pallas_call | solution.py:311
  111.8 59.4 %all_to_all.25.own_ref = f32[64,128,128]{2,1,0:T(8,128)} all-to-all(f32[64,128,128]{2,1,0:T(8,128)} %get-tuple-element.27), channel_id=1, replica_groups=mesh['sub'=2,'y'=4,'core'=2,'xlo'=2,'z'=4] {'sub','y','xlo','z'}, dimensions={0} | all-to-all | bytes 8388608 | tf_op jit(solution)/shard_map/all_to_all | solution.py:448
  171.2 2.3 collective-permute-start.1
  175.0 5.6 %collective-permute-done.1.other_ref = f32[64,128,128]{2,1,0:T(8,128)} collective-permute-done((f32[64,128,128]{2,1,0:T(8,128)}, f32[64,128,128]{2,1,0:T(8,128)}, u32[]{:S(2)}, u32[]{:S(2)}) %collective-permute-start.1) | collective-permute-done | bytes 4194336 | tf_op jit(solution)/shard_map/ppermute | solution.py:449
  180.7 7.8 %assemble.1.front_ref = f32[768,1536]{1,0:T(8,128)} custom-call(s32[12]{0:T(128)} %reshape.43.rows_ref, s32[24]{0:T(128)} %reshape.44.cols_ref, f32[768,1536]{1,0:T(8,128)} %front_ref.1, f32[64,128,128]{2,1,0:T(8,128)} %all_to_all.25.own_ref, f32[64,128,128]{2,1,0:T(8,128)} %collective-permute-done.1.other_ref), custom_call_target="tpu_custom_call" | custom-call | tf_op jit(solution)/shard_map/assemble/pallas_call | solution.py:399
  189.2 0.9 fusion.11
  191.8 1.3 collective-permute-start.4
  193.1 1.8 collective-permute-done.4
  195.0 1.2 broadcast_in_dim.66
  196.2 7.1 %all-to-all-start.3 = ((f32[64,40,128]{2,1,0:T(8,128)}), f32[64,40,128]{2,1,0:T(8,128)}, u32[]{:S(2)}, u32[]{:S(2)}) async-start(f32[64,40,128]{2,1,0:T(8,128)} %broadcast_in_dim.66), calls=%async_computation.3 | async-start | bytes 2621440 | tf_op jit(solution)/shard_map/all_to_all | solution.py:415
  203.3 1.2 fusion.12
  204.5 1.3 collective-permute-start.2
  205.8 2.3 collective-permute-done.2
  208.2 2.6 collective-permute-start.3
  210.8 16.8 %collective-permute-done.3 = f32[64,1408]{1,0:T(8,128)S(1)} collective-permute-done((f32[64,1408]{1,0:T(8,128)S(1)}, f32[64,1408]{1,0:T(8,128)S(1)}, u32[]{:S(2)}, u32[]{:S(2)}) %collective-permute-start.3) | collective-permute-done | bytes 360480 | tf_op jit(solution)/shard_map/ppermute | solution.py:465
  228.6 1.4 collective-permute-start.5
  230.0 1.9 broadcast_in_dim.67
  231.9 4.0 %all-to-all-start.4 = ((f32[8,768,128]{2,1,0:T(8,128)}), f32[8,768,128]{2,1,0:T(8,128)S(1)}, u32[]{:S(2)}, u32[]{:S(2)}) async-start(f32[8,768,128]{2,1,0:T(8,128)} %broadcast_in_dim.67), calls=%async_computation.4 | async-start | bytes 6291456 | tf_op jit(solution)/shard_map/all_to_all | solution.py:415
  237.1 37.8 %factor.3 = (bf16[1024,1024]{1,0:T(8,128)(2,1)}, bf16[1024,1024]{1,0:T(8,128)(2,1)}, f32[128,128]{1,0:T(8,128)}) custom-call(s32[3]{0:T(128)} %add_add_fusion.1.where_ref, f32[8,8,40,128]{3,2,1,0:T(8,128)} %bitcast.12.own_ref, f32[8,8,40,128]{3,2,1,0:T(8,128)} %collective-permute-done.5.other_ref), custom_call_target="tpu_custom_call" | custom-call | flops 20000000000 | bytes 16777216 | tf_op jit(solution)/shard_map/factor/pallas_call | solution.py:210
  275.0 1.7 copy-done
  276.7 24.9 %parent_update.1 = (f32[768,1536]{1,0:T(8,128)}, f32[768,128]{1,0:T(8,128)}) custom-call(s32[2]{0:T(128)} %pad_add_fusion.1.where_ref, f32[768,1536]{1,0:T(8,128)} %assemble.1.front_ref, f32[8,768,128]{2,1,0:T(8,128)} %copy-done, f32[8,2,64,1408]{3,2,1,0:T(8,128)} %bitcast.37, bf16[1024,1024]{1,0:T(8,128)(2,1)} %get-tuple-element.33.x_high_ref, ...), custom_call_target="tpu_custom_call" | custom-call | tf_op jit(solution)/shard_map/parent_update/pallas_call | solution.py:351
  (55 shorter events, 11.0 us)
Async XLA Ops:
  11.6 26.7 %all-to-all-start = ((f32[32,72,128]{2,1,0:T(8,128)}), f32[32,72,128]{2,1,0:T(8,128)S(1)}, u32[]{:S(2)}, u32[]{:S(2)}) async-start(f32[32,72,128]{2,1,0:T(8,128)} %broadcast_in_dim.61), calls=%async_computation | async-start | bytes 2359296 | tf_op jit(solution)/shard_map/all_to_all | solution.py:415
  21.4 68.5 %all-gather.4.cloned.1.call-start = ((), (), s32[]{:S(2)}) async-start(), calls=%async_computation.5 | async-start | bytes 4128768 | tf_op jit(solution)/shard_map/all_gather | solution.py:433
  38.3 8.2 %copy-start.1 = (f32[32,72,128]{2,1,0:T(8,128)}, f32[32,72,128]{2,1,0:T(8,128)S(1)}, u32[]{:S(2)}) copy-start(f32[32,72,128]{2,1,0:T(8,128)S(1)} %all-to-all-done) | copy-start | bytes 3538948
  41.8 6.6 %copy-start.2 = (s32[2,56]{1,0:T(2,128)S(1)}, s32[2,56]{1,0:T(2,128)}, u32[]{:S(2)}) copy-start(s32[2,56]{1,0:T(2,128)} %param.4) | copy-start | bytes 1348
  41.8 48.0 %all-to-all-start.1 = ((f32[8,896,128]{2,1,0:T(8,128)}), f32[8,896,128]{2,1,0:T(8,128)}, u32[]{:S(2)}, u32[]{:S(2)}) async-start(f32[8,896,128]{2,1,0:T(8,128)} %broadcast_in_dim.35), calls=%async_computation.1 | async-start | bytes 7340032 | tf_op jit(solution)/shard_map/all_to_all | solution.py:415
  46.5 5.1 %collective-permute-start = (f32[4,8,72,128]{3,2,1,0:T(8,128)S(1)}, f32[4,8,72,128]{3,2,1,0:T(8,128)S(1)}, u32[]{:S(2)}, u32[]{:S(2)}) collective-permute-start(f32[4,8,72,128]{3,2,1,0:T(8,128)S(1)} %bitcast.38), channel_id=1, source_target_pairs={{0,8},{8,0},{1,9},{9,1},{2,10},{10,2},{3,11},{11,3},{4,12},{12,4},... | collective-permute-start | bytes 3538952 | tf_op jit(solution)/shard_map/ppermute | solution.py:434
  51.6 1.0 copy-start.3
  171.2 9.4 %collective-permute-start.1 = (f32[64,128,128]{2,1,0:T(8,128)}, f32[64,128,128]{2,1,0:T(8,128)}, u32[]{:S(2)}, u32[]{:S(2)}) collective-permute-start(f32[64,128,128]{2,1,0:T(8,128)} %all_to_all.25.own_ref), channel_id=1, source_target_pairs={{0,8},{8,0},{1,9},{9,1},{2,10},{10,2},{3,11},{11,3},{4,12},{12,4},... | collective-permute-start | bytes 12582920 | tf_op jit(solution)/shard_map/ppermute | solution.py:449
  191.8 3.1 %collective-permute-start.4 = (f32[40,128]{0,1:T(8,128)S(1)}, f32[40,128]{0,1:T(8,128)S(1)}, u32[]{:S(2)}, u32[]{:S(2)}) collective-permute-start(f32[40,128]{0,1:T(8,128)S(1)} %pad_maximum_fusion.1), channel_id=1, source_target_pairs={{0,8},{1,9},{2,10},{3,11},{4,12},{5,13},{6,14},{7,15},{16,24},{17,... | collective-permute-start | bytes 61448 | tf_op jit(solution)/shard_map/ppermute | solution.py:468
  196.2 31.5 %all-to-all-start.3 = ((f32[64,40,128]{2,1,0:T(8,128)}), f32[64,40,128]{2,1,0:T(8,128)}, u32[]{:S(2)}, u32[]{:S(2)}) async-start(f32[64,40,128]{2,1,0:T(8,128)} %broadcast_in_dim.66), calls=%async_computation.3 | async-start | bytes 2621440 | tf_op jit(solution)/shard_map/all_to_all | solution.py:415
  203.3 26.7 %slice-start = ((f32[768,1536]{1,0:T(8,128)}), f32[768,128]{1,0:T(8,128)S(1)}, s32[]{:S(2)}) async-start(f32[768,1536]{1,0:T(8,128)} %assemble.1.front_ref), calls=%async_computation.7 | async-start | bytes 786432 | tf_op jit(solution)/shard_map/slice | solution.py:474
  203.3 71.7 %all-gather.6.cloned.1.call-start = ((), (), s32[]{:S(2)}) async-start(), calls=%async_computation.6 | async-start | bytes 6488064 | tf_op jit(solution)/shard_map/all_gather | solution.py:473
  204.5 3.6 %collective-permute-start.2 = (f32[64,1536]{1,0:T(8,128)S(1)}, f32[64,1536]{1,0:T(8,128)S(1)}, u32[]{:S(2)}, u32[]{:S(2)}) collective-permute-start(f32[64,1536]{1,0:T(8,128)S(1)} %get-tuple-element.41), channel_id=1, source_target_pairs={{0,8},{1,9},{2,10},{3,11},{4,12},{5,13},{6,14},{7,15},{16,24},{17,... | collective-permute-start | bytes 1179656 | tf_op jit(solution)/shard_map/ppermute | solution.py:464
  208.2 19.4 %collective-permute-start.3 = (f32[64,1408]{1,0:T(8,128)S(1)}, f32[64,1408]{1,0:T(8,128)S(1)}, u32[]{:S(2)}, u32[]{:S(2)}) collective-permute-start(f32[64,1408]{1,0:T(8,128)S(1)} %slice_select_fusion), channel_id=1, source_target_pairs={{0,64},{64,0},{1,65},{65,1},{2,66},{66,2},{3,67},{67,3},{4,68},{68... | collective-permute-start | bytes 1081352 | tf_op jit(solution)/shard_map/ppermute | solution.py:465
  228.6 8.5 %collective-permute-start.5 = (f32[8,8,40,128]{3,2,1,0:T(8,128)}, f32[8,8,40,128]{3,2,1,0:T(8,128)}, u32[]{:S(2)}, u32[]{:S(2)}) collective-permute-start(f32[8,8,40,128]{3,2,1,0:T(8,128)} %bitcast.12.own_ref), channel_id=1, source_target_pairs={{0,8},{8,0},{1,9},{9,1},{2,10},{10,2},{3,11},{11,3},{4,12},{12,4},... | collective-permute-start | bytes 3932168 | tf_op jit(solution)/shard_map/ppermute | solution.py:470
  231.9 43.0 %all-to-all-start.4 = ((f32[8,768,128]{2,1,0:T(8,128)}), f32[8,768,128]{2,1,0:T(8,128)S(1)}, u32[]{:S(2)}, u32[]{:S(2)}) async-start(f32[8,768,128]{2,1,0:T(8,128)} %broadcast_in_dim.67), calls=%async_computation.4 | async-start | bytes 6291456 | tf_op jit(solution)/shard_map/all_to_all | solution.py:415
  274.9 1.8 copy-start
Sparse Core Ops, SparseCore 0:
  38.5 30.2 all-gather.3
  228.8 38.8 all-gather.5

commit v2 on v1

--- a/solution.py
+++ b/solution.py
@@ -81,11 +81,24 @@
                 for m in range(k + 1, 8):
                     row = row - c[k][m] * q[m]
                 q[k] = row * root[k]
-            for i in range(p + 2, count):
+            near = p + 3 + (count - p - 3) % 2
+            for i in range(p + 2, min(near, count)):
                 new = jnp.where(inside, 0.0, s[i])
                 for k in range(8):
                     new = new - jnp.broadcast_to(s[i][:, j0 + k : j0 + k + 1], full) * q[k]
                 s[i] = new
+            if near < count:
+                eight = jnp.zeros(full, jnp.float32)
+                for k in range(8):
+                    eight = jnp.where(sub == k, q[k], eight)
+                zeros = [jnp.zeros((j0, TILE), jnp.float32)] if p else []
+                right = jnp.concatenate(zeros + [eight, jnp.zeros((TILE - 8 - j0, TILE), jnp.float32)], 0)
+                rest = jnp.concatenate(s[near:], 0)
+                within = jnp.concatenate([inside] * (count - near), 0)
+                product = dot3(split(jnp.where(within, rest, 0.0)), split(right), ((1,), (0,)))
+                rest = jnp.where(within, 0.0, rest) - product
+                for i in range(near, count):
+                    s[i] = rest[8 * (i - near) : 8 * (i - near) + 8]
         if more:
             s[p + 1] = later
         out = jnp.zeros(full, jnp.float32)

time: 315 us -> 311 us (0.987)
  Pallas kernels: 130 us -> 120 us
  waiting for transfers between devices: 43.5 us -> 50.8 us
    pallas_call x2, Pallas kernels: 75 us -> 65.7 us  [factor(): pl.pallas_call(factor_kernel, out_shape=(jax.ShapeDtypeStruct((ORDER, ORD...]
    all_to_all x4, waiting for transfers between devices: 15 us -> 22.4 us  [spread(): return lax.all_to_all(copies, axes, 0, 0, tiled=True)]
  transfers between devices with their start and end apart: 12 -> 12, of which waited for: 6 -> 8; matrix products, arithmetic and copies ran while one was open for 4% -> 4% of each run, Pallas kernels for 24% -> 22%
where the time goes in v2:
time: 311 us; the launch traced here: 305 us
  Pallas kernels  120 us (39%)
  blocking collectives  57.9 us (19%)
  waiting for transfers between devices  50.8 us (16%)
  starting transfers between devices  36.8 us (12%)
  local copies, waits for them, and re-layouts  19.1 us (6%)
  between operations  14.5 us (5%)
  other arithmetic  6.06 us (2%)
    pallas_call x2, Pallas kernels, factor(): pl.pallas_call(factor_kernel, out_shape=(jax.ShapeDtypeStruct((ORDER, ORD...  65.7 us
    all_to_all x1, blocking collectives, local(): box = lax.all_to_all(box, GROUP + COL, 0, 0, tiled=True)  57.9 us
    all_to_all x4, starting transfers between devices, spread(): return lax.all_to_all(copies, axes, 0, 0, tiled=True)  25.5 us
    pallas_call x1, Pallas kernels, parent_update(): pl.pallas_call(parent_kernel, out_shape=(jax.ShapeDtypeStruct(front.shape...  24.9 us
    all_to_all x4, waiting for transfers between devices, spread(): return lax.all_to_all(copies, axes, 0, 0, tiled=True)  22.4 us
    pallas_call x1, Pallas kernels, child_update(): pl.pallas_call(child_kernel, out_shape=(jax.ShapeDtypeStruct((STEPS * STE...  21.9 us
    ppermute x1, waiting for transfers between devices, local(): strip_other = lax.ppermute(strip[:, TILE:], 'sub', SWAP)  16.8 us
    pallas_call x1, Pallas kernels, assemble(): pl.pallas_call(assemble_kernel, out_shape=jax.ShapeDtypeStruct(front.shap...  7.54 us
  transfers between devices with their start and end apart: 12, of which 8 were waited for; matrix products, arithmetic and copies ran while one was open for 4% of the time, Pallas kernels for 22%

profile of v2, /device:TPU:1, one launch (start us, length us, event | category | flops | bytes accessed | tf_op | source)
XLA Modules:
  0.0 305.2 jit_solution(15331553006153818647)
XLA Ops:
  10.5 1.1 broadcast_in_dim.61
  11.6 9.8 %all-to-all-start = ((f32[32,72,128]{2,1,0:T(8,128)}), f32[32,72,128]{2,1,0:T(8,128)S(1)}, u32[]{:S(2)}, u32[]{:S(2)}) async-start(f32[32,72,128]{2,1,0:T(8,128)} %broadcast_in_dim.61), calls=%async_computation | async-start | bytes 2359296 | tf_op jit(solution)/shard_map/all_to_all | solution.py:428
  21.5 1.8 slice.96
  23.3 15.0 %all-to-all-done = f32[32,72,128]{2,1,0:T(8,128)S(1)} async-done(((f32[32,72,128]{2,1,0:T(8,128)}), f32[32,72,128]{2,1,0:T(8,128)S(1)}, u32[]{:S(2)}, u32[]{:S(2)}) %all-to-all-start) | async-done | bytes 1179680 | tf_op jit(solution)/shard_map/all_to_all | solution.py:428
  38.3 1.4 slice.90
  39.8 2.1 broadcast_in_dim.35
  41.8 4.7 %all-to-all-start.1 = ((f32[8,896,128]{2,1,0:T(8,128)}), f32[8,896,128]{2,1,0:T(8,128)}, u32[]{:S(2)}, u32[]{:S(2)}) async-start(f32[8,896,128]{2,1,0:T(8,128)} %broadcast_in_dim.35), calls=%async_computation.1 | async-start | bytes 7340032 | tf_op jit(solution)/shard_map/all_to_all | solution.py:428
  46.5 1.9 collective-permute-start
  49.8 1.8 collective-permute-done.other_ref
  52.6 32.6 %factor.2 = (bf16[1024,1024]{1,0:T(8,128)(2,1)}, bf16[1024,1024]{1,0:T(8,128)(2,1)}, f32[128,128]{1,0:T(8,128)}) custom-call(s32[3]{0:T(128)} %add_add_fusion.where_ref, f32[4,8,72,128]{3,2,1,0:T(8,128)} %bitcast.39, f32[4,8,72,128]{3,2,1,0:T(8,128)} %copy-done.3), custom_call_target="tpu_custom_call" | custom-call | flops 20000000000 | bytes 16777216 | tf_op jit(solution)/shard_map/factor/pallas_call | solution.py:223
  85.2 4.3 %all-to-all-done.1.cols_ref = f32[8,896,128]{2,1,0:T(8,128)} async-done(((f32[8,896,128]{2,1,0:T(8,128)}), f32[8,896,128]{2,1,0:T(8,128)}, u32[]{:S(2)}, u32[]{:S(2)}) %all-to-all-start.1) | async-done | bytes 3670048 | tf_op jit(solution)/shard_map/all_to_all | solution.py:428
  89.5 21.9 %child_update.1 = (f32[64,128,128]{2,1,0:T(8,128)}, f32[1024,128]{1,0:T(8,128)}) custom-call(s32[15]{0:T(128)} %pad_add_fusion.where_ref, f32[1024,1024]{1,0:T(8,128)} %bitcast.36, f32[8,896,128]{2,1,0:T(8,128)} %all-to-all-done.1.cols_ref, f32[1024,896]{1,0:T(8,128)} %all-gather.4.cloned.1.call-done.rows_ref, ...), custom_call_target="tpu_custom_call" | custom-call | tf_op jit(solution)/shard_map/child_update/pallas_call | solution.py:324
  111.4 57.9 %all_to_all.25.own_ref = f32[64,128,128]{2,1,0:T(8,128)} all-to-all(f32[64,128,128]{2,1,0:T(8,128)} %get-tuple-element.27), channel_id=1, replica_groups=mesh['sub'=2,'y'=4,'core'=2,'xlo'=2,'z'=4] {'sub','y','xlo','z'}, dimensions={0} | all-to-all | bytes 8388608 | tf_op jit(solution)/shard_map/all_to_all | solution.py:461
  169.3 2.7 collective-permute-start.1
  173.5 5.6 %collective-permute-done.1.other_ref = f32[64,128,128]{2,1,0:T(8,128)} collective-permute-done((f32[64,128,128]{2,1,0:T(8,128)}, f32[64,128,128]{2,1,0:T(8,128)}, u32[]{:S(2)}, u32[]{:S(2)}) %collective-permute-start.1) | collective-permute-done | bytes 4194336 | tf_op jit(solution)/shard_map/ppermute | solution.py:462
  179.1 7.5 %assemble.1.front_ref = f32[768,1536]{1,0:T(8,128)} custom-call(s32[12]{0:T(128)} %reshape.43.rows_ref, s32[24]{0:T(128)} %reshape.44.cols_ref, f32[768,1536]{1,0:T(8,128)} %front_ref.1, f32[64,128,128]{2,1,0:T(8,128)} %all_to_all.25.own_ref, f32[64,128,128]{2,1,0:T(8,128)} %collective-permute-done.1.other_ref), custom_call_target="tpu_custom_call" | custom-call | tf_op jit(solution)/shard_map/assemble/pallas_call | solution.py:412
  190.0 1.3 collective-permute-start.4
  191.3 1.8 collective-permute-done.4
  193.2 1.2 broadcast_in_dim.66
  194.3 7.0 %all-to-all-start.3 = ((f32[64,40,128]{2,1,0:T(8,128)}), f32[64,40,128]{2,1,0:T(8,128)}, u32[]{:S(2)}, u32[]{:S(2)}) async-start(f32[64,40,128]{2,1,0:T(8,128)} %broadcast_in_dim.66), calls=%async_computation.3 | async-start | bytes 2621440 | tf_op jit(solution)/shard_map/all_to_all | solution.py:428
  201.4 1.2 fusion.12
  202.6 1.3 collective-permute-start.2
  203.9 2.3 collective-permute-done.2
  206.3 2.6 collective-permute-start.3
  208.9 16.8 %collective-permute-done.3 = f32[64,1408]{1,0:T(8,128)S(1)} collective-permute-done((f32[64,1408]{1,0:T(8,128)S(1)}, f32[64,1408]{1,0:T(8,128)S(1)}, u32[]{:S(2)}, u32[]{:S(2)}) %collective-permute-start.3) | collective-permute-done | bytes 360480 | tf_op jit(solution)/shard_map/ppermute | solution.py:478
  226.7 1.4 collective-permute-start.5
  228.1 1.9 broadcast_in_dim.67
  230.0 4.0 %all-to-all-start.4 = ((f32[8,768,128]{2,1,0:T(8,128)}), f32[8,768,128]{2,1,0:T(8,128)S(1)}, u32[]{:S(2)}, u32[]{:S(2)}) async-start(f32[8,768,128]{2,1,0:T(8,128)} %broadcast_in_dim.67), calls=%async_computation.4 | async-start | bytes 6291456 | tf_op jit(solution)/shard_map/all_to_all | solution.py:428
  235.2 33.1 %factor.3 = (bf16[1024,1024]{1,0:T(8,128)(2,1)}, bf16[1024,1024]{1,0:T(8,128)(2,1)}, f32[128,128]{1,0:T(8,128)}) custom-call(s32[3]{0:T(128)} %add_add_fusion.1.where_ref, f32[8,8,40,128]{3,2,1,0:T(8,128)} %bitcast.12.own_ref, f32[8,8,40,128]{3,2,1,0:T(8,128)} %collective-permute-done.5.other_ref), custom_call_target="tpu_custom_call" | custom-call | flops 20000000000 | bytes 16777216 | tf_op jit(solution)/shard_map/factor/pallas_call | solution.py:223
  268.3 3.1 %all-to-all-done.4.cols_ref = f32[8,768,128]{2,1,0:T(8,128)S(1)} async-done(((f32[8,768,128]{2,1,0:T(8,128)}), f32[8,768,128]{2,1,0:T(8,128)S(1)}, u32[]{:S(2)}, u32[]{:S(2)}) %all-to-all-start.4) | async-done | bytes 3145760 | tf_op jit(solution)/shard_map/all_to_all | solution.py:428
  271.4 1.8 copy-done
  273.2 24.9 %parent_update.1 = (f32[768,1536]{1,0:T(8,128)}, f32[768,128]{1,0:T(8,128)}) custom-call(s32[2]{0:T(128)} %pad_add_fusion.1.where_ref, f32[768,1536]{1,0:T(8,128)} %assemble.1.front_ref, f32[8,768,128]{2,1,0:T(8,128)} %copy-done, f32[8,2,64,1408]{3,2,1,0:T(8,128)} %bitcast.37, bf16[1024,1024]{1,0:T(8,128)(2,1)} %get-tuple-element.33.x_high_ref, ...), custom_call_target="tpu_custom_call" | custom-call | tf_op jit(solution)/shard_map/parent_update/pallas_call | solution.py:364
  (55 shorter events, 12.9 us)
Async XLA Ops:
  11.6 26.7 %all-to-all-start = ((f32[32,72,128]{2,1,0:T(8,128)}), f32[32,72,128]{2,1,0:T(8,128)S(1)}, u32[]{:S(2)}, u32[]{:S(2)}) async-start(f32[32,72,128]{2,1,0:T(8,128)} %broadcast_in_dim.61), calls=%async_computation | async-start | bytes 2359296 | tf_op jit(solution)/shard_map/all_to_all | solution.py:428
  21.4 68.0 %all-gather.4.cloned.1.call-start = ((), (), s32[]{:S(2)}) async-start(), calls=%async_computation.5 | async-start | bytes 4128768 | tf_op jit(solution)/shard_map/all_gather | solution.py:446
  38.3 8.2 %copy-start.1 = (f32[32,72,128]{2,1,0:T(8,128)}, f32[32,72,128]{2,1,0:T(8,128)S(1)}, u32[]{:S(2)}) copy-start(f32[32,72,128]{2,1,0:T(8,128)S(1)} %all-to-all-done) | copy-start | bytes 3538948
  41.8 6.6 %copy-start.2 = (s32[2,56]{1,0:T(2,128)S(1)}, s32[2,56]{1,0:T(2,128)}, u32[]{:S(2)}) copy-start(s32[2,56]{1,0:T(2,128)} %param.4) | copy-start | bytes 1348
  41.8 47.6 %all-to-all-start.1 = ((f32[8,896,128]{2,1,0:T(8,128)}), f32[8,896,128]{2,1,0:T(8,128)}, u32[]{:S(2)}, u32[]{:S(2)}) async-start(f32[8,896,128]{2,1,0:T(8,128)} %broadcast_in_dim.35), calls=%async_computation.1 | async-start | bytes 7340032 | tf_op jit(solution)/shard_map/all_to_all | solution.py:428
  46.5 5.1 %collective-permute-start = (f32[4,8,72,128]{3,2,1,0:T(8,128)S(1)}, f32[4,8,72,128]{3,2,1,0:T(8,128)S(1)}, u32[]{:S(2)}, u32[]{:S(2)}) collective-permute-start(f32[4,8,72,128]{3,2,1,0:T(8,128)S(1)} %bitcast.38), channel_id=1, source_target_pairs={{0,8},{8,0},{1,9},{9,1},{2,10},{10,2},{3,11},{11,3},{4,12},{12,4},... | collective-permute-start | bytes 3538952 | tf_op jit(solution)/shard_map/ppermute | solution.py:447
  51.6 1.0 copy-start.3
  169.3 9.8 %collective-permute-start.1 = (f32[64,128,128]{2,1,0:T(8,128)}, f32[64,128,128]{2,1,0:T(8,128)}, u32[]{:S(2)}, u32[]{:S(2)}) collective-permute-start(f32[64,128,128]{2,1,0:T(8,128)} %all_to_all.25.own_ref), channel_id=1, source_target_pairs={{0,8},{8,0},{1,9},{9,1},{2,10},{10,2},{3,11},{11,3},{4,12},{12,4},... | collective-permute-start | bytes 12582920 | tf_op jit(solution)/shard_map/ppermute | solution.py:462
  190.0 3.1 %collective-permute-start.4 = (f32[40,128]{0,1:T(8,128)S(1)}, f32[40,128]{0,1:T(8,128)S(1)}, u32[]{:S(2)}, u32[]{:S(2)}) collective-permute-start(f32[40,128]{0,1:T(8,128)S(1)} %pad_maximum_fusion.1), channel_id=1, source_target_pairs={{0,8},{1,9},{2,10},{3,11},{4,12},{5,13},{6,14},{7,15},{16,24},{17,... | collective-permute-start | bytes 61448 | tf_op jit(solution)/shard_map/ppermute | solution.py:481
  194.3 31.4 %all-to-all-start.3 = ((f32[64,40,128]{2,1,0:T(8,128)}), f32[64,40,128]{2,1,0:T(8,128)}, u32[]{:S(2)}, u32[]{:S(2)}) async-start(f32[64,40,128]{2,1,0:T(8,128)} %broadcast_in_dim.66), calls=%async_computation.3 | async-start | bytes 2621440 | tf_op jit(solution)/shard_map/all_to_all | solution.py:428
  201.4 26.7 %slice-start = ((f32[768,1536]{1,0:T(8,128)}), f32[768,128]{1,0:T(8,128)S(1)}, s32[]{:S(2)}) async-start(f32[768,1536]{1,0:T(8,128)} %assemble.1.front_ref), calls=%async_computation.7 | async-start | bytes 786432 | tf_op jit(solution)/shard_map/slice | solution.py:487
  201.4 70.1 %all-gather.6.cloned.1.call-start = ((), (), s32[]{:S(2)}) async-start(), calls=%async_computation.6 | async-start | bytes 6488064 | tf_op jit(solution)/shard_map/all_gather | solution.py:486
  202.6 3.6 %collective-permute-start.2 = (f32[64,1536]{1,0:T(8,128)S(1)}, f32[64,1536]{1,0:T(8,128)S(1)}, u32[]{:S(2)}, u32[]{:S(2)}) collective-permute-start(f32[64,1536]{1,0:T(8,128)S(1)} %get-tuple-element.41), channel_id=1, source_target_pairs={{0,8},{1,9},{2,10},{3,11},{4,12},{5,13},{6,14},{7,15},{16,24},{17,... | collective-permute-start | bytes 1179656 | tf_op jit(solution)/shard_map/ppermute | solution.py:477
  206.3 19.4 %collective-permute-start.3 = (f32[64,1408]{1,0:T(8,128)S(1)}, f32[64,1408]{1,0:T(8,128)S(1)}, u32[]{:S(2)}, u32[]{:S(2)}) collective-permute-start(f32[64,1408]{1,0:T(8,128)S(1)} %slice_select_fusion), channel_id=1, source_target_pairs={{0,64},{64,0},{1,65},{65,1},{2,66},{66,2},{3,67},{67,3},{4,68},{68... | collective-permute-start | bytes 1081352 | tf_op jit(solution)/shard_map/ppermute | solution.py:478
  226.7 8.5 %collective-permute-start.5 = (f32[8,8,40,128]{3,2,1,0:T(8,128)}, f32[8,8,40,128]{3,2,1,0:T(8,128)}, u32[]{:S(2)}, u32[]{:S(2)}) collective-permute-start(f32[8,8,40,128]{3,2,1,0:T(8,128)} %bitcast.12.own_ref), channel_id=1, source_target_pairs={{0,8},{8,0},{1,9},{9,1},{2,10},{10,2},{3,11},{11,3},{4,12},{12,4},... | collective-permute-start | bytes 3932168 | tf_op jit(solution)/shard_map/ppermute | solution.py:483
  230.0 41.5 %all-to-all-start.4 = ((f32[8,768,128]{2,1,0:T(8,128)}), f32[8,768,128]{2,1,0:T(8,128)S(1)}, u32[]{:S(2)}, u32[]{:S(2)}) async-start(f32[8,768,128]{2,1,0:T(8,128)} %broadcast_in_dim.67), calls=%async_computation.4 | async-start | bytes 6291456 | tf_op jit(solution)/shard_map/all_to_all | solution.py:428
  271.4 1.8 copy-start
Sparse Core Ops, SparseCore 0:
  38.5 30.2 all-gather.3
  226.8 38.8 all-gather.5
